TPU v7x, 32 devices: a whole 2x2x4 slice. The times are simulated.
32 devices in a mesh: slab: 8 (over y, x, core), field: 4 (over z).
Axes of the slice: x: 2, y: 2, z: 4, core: 2. Of those that a mesh axis runs over, the one named last changes fastest.
Arguments:
- snaps: bfloat16 [4, 16, 3, 32, 2048], P('field', 'slab'), may hold values from -6 to 6
- writer_map: int32 [64], replicated, may hold values from 0 to 63, each once
- omega: int32 [64, 64], replicated, may hold values from -3 to 3
- face_level: int32 [32], replicated, may hold values from 0 to 11
Outputs:
- sketch_rows: float32 [4, 16, 64], P('field')
- core: float32 [64, 64], replicated
All inputs are finite; a program needn't handle non-finite values.
Results may differ from a plain program's by a relative error of at most 0.00035.
Values may be sent and summed in bfloat16 or wider, within the bound.
A program may use at most 128 MiB of HBM per device.

v0:
```python
import jax
import jax.numpy as jnp
from jax import lax
from jax.sharding import PartitionSpec as P


def from_behind(block, axis, distance):
    devices = range(lax.axis_size(axis))
    route = [(i - distance, i) for i in devices if i - distance in devices]
    return lax.ppermute(block, axis, route)


def body(snaps, writer_map, omega, face_level):
    field_count = lax.axis_size("field")
    slab_at = lax.axis_index("slab")
    field_at = lax.axis_index("field")
    sketch_cols = omega.shape[1]
    total_snaps = omega.shape[0]
    total_planes = face_level.shape[0]
    group_rows = total_snaps // field_count
    columns = jnp.arange(total_snaps, dtype=jnp.int32)
    onehot = (writer_map[:, None] == columns[None, :]).astype(jnp.bfloat16)
    test_all = jnp.dot(
        onehot, omega.astype(jnp.bfloat16), preferred_element_type=jnp.float32
    ).astype(jnp.bfloat16)
    local = lax.all_to_all(snaps, "slab", split_axis=3, concat_axis=1, tiled=True)
    comps = local.shape[2]
    planes_dev = local.shape[3]
    cells = local.shape[4]
    features = comps * planes_dev * cells
    test_own = lax.dynamic_slice_in_dim(test_all, field_at * group_rows, group_rows, 0)
    flat = local.reshape(group_rows, features)
    partial_z = jnp.dot(test_own.T, flat, preferred_element_type=jnp.float32)
    sketched = lax.psum(partial_z.astype(jnp.bfloat16), "field").astype(jnp.float32)
    sketched = sketched.reshape(sketch_cols, comps, planes_dev, cells)
    spacing = 0.5 * jnp.power(jnp.float32(1.12), face_level.astype(jnp.float32))
    first_plane = slab_at * planes_dev
    weight = lax.dynamic_slice_in_dim(spacing, first_plane, planes_dev, 0).reshape(
        1, 1, planes_dev, 1
    )
    coupling = lax.dynamic_slice_in_dim(1.0 / spacing, first_plane, planes_dev, 0).reshape(
        1, 1, planes_dev, 1
    )
    scale = 1.0 / (comps * total_planes * cells)
    lower = from_behind(
        sketched[:, :, -1:].astype(jnp.bfloat16), ("slab", "field"), field_count
    ).astype(jnp.float32)
    below = jnp.concatenate([lower, sketched[:, :, :-1]], axis=2)
    flux = coupling * (sketched - below)
    upper = from_behind(
        flux[:, :, :1].astype(jnp.bfloat16), ("slab", "field"), -field_count
    ).astype(jnp.float32)
    above = jnp.concatenate([flux[:, :, 1:], upper], axis=2)
    applied = (
        ((weight * sketched + flux - above) * scale)
        .astype(jnp.bfloat16)
        .reshape(sketch_cols, features)
    )
    partial_rows = lax.dot_general(
        flat, applied, (((1,), (1,)), ((), ())), preferred_element_type=jnp.float32
    )
    blocks = (jnp.arange(field_count, dtype=jnp.int32) == field_at).astype(jnp.float32)
    stored_rows = (blocks[:, None, None] * partial_rows[None, :, :]).reshape(
        total_snaps, sketch_cols
    )
    rows = lax.psum(stored_rows, ("slab", "field"))
    core = (
        jnp.dot(test_all.astype(jnp.float32).T, rows, precision=lax.Precision.HIGHEST) / total_snaps
    )
    own_rows = lax.dynamic_slice_in_dim(rows, field_at * group_rows, group_rows, 0)
    return (own_rows.reshape(1, group_rows, sketch_cols), core)


def solution(mesh):
    in_specs = (P("field", "slab", None, None, None), P(), P(), P())
    out_specs = (P("field", None, None), P())
    return jax.shard_map(body, mesh=mesh, in_specs=in_specs, out_specs=out_specs, check_vma=False)
```

profile of v0, /device:TPU:0, one launch (start us, length us, event | category | flops | bytes accessed | tf_op | source)
XLA Modules:
  0.0 285.8 jit_solution(11686878091657337957)
XLA Ops:
  7.2 2.8 copy.7
  10.0 5.2 %all-to-all-start = ((bf16[1,2,3,32,2048]{4,2,1,0,3:T(4,128)(2,1)}), bf16[1,2,3,32,2048]{4,2,1,0,3:T(4,128)(2,1)S(1)}, u32[]{:S(2)}, u32[]{:S(2)}) async-start(bf16[1,2,3,32,2048]{4,2,1,0,3:T(4,128)(2,1)} %copy.7), calls=%async_computation | async-start | bytes 2097152 | tf_op jit(solution)/shard_map/all_to_all | solution.py:26
  15.2 1.0 convolution_convert_fusion.1
  16.2 14.4 %all-to-all-done = bf16[1,2,3,32,2048]{4,2,1,0,3:T(4,128)(2,1)S(1)} async-done(((bf16[1,2,3,32,2048]{4,2,1,0,3:T(4,128)(2,1)}), bf16[1,2,3,32,2048]{4,2,1,0,3:T(4,128)(2,1)S(1)}, u32[]{:S(2)}, u32[]{:S(2)}) %all-to-all-start) | async-done | bytes 786464 | tf_op jit(solution)/shard_map/all_to_all | solution.py:26
  30.5 0.9 copy.18
  32.1 2.7 convolution_convert_fusion
  34.8 120.6 %all-reduce.2.cloned.1.call-done = bf16[64,24576]{1,0:T(8,128)(2,1)} async-done(((bf16[64,24576]{1,0:T(8,128)(2,1)}), bf16[64,24576]{1,0:T(8,128)(2,1)}) %all-reduce.2.cloned.1.call-update) | async-done | bytes 3145744 | tf_op jit(solution)/shard_map/psum | solution.py:34
  155.4 7.9 %reshape.34 = f32[64,3,4,2048]{3,2,1,0:T(4,128)} reshape(bf16[64,24576]{1,0:T(8,128)(2,1)} %all-reduce.2.cloned.1.call-done) | data formatting | bytes 9437184 | tf_op jit(solution)/shard_map/reshape | solution.py:35
  163.3 4.5 %slice.25 = bf16[64,3,1,2048]{3,2,1,0:T(2,128)(2,1)S(1)} slice(f32[64,3,4,2048]{3,2,1,0:T(4,128)} %reshape.34), slice={[0:64], [0:3], [3:4], [0:2048]} | slice | bytes 1572864 | tf_op jit(solution)/shard_map/slice | solution.py:46
  168.2 1.9 collective-permute-start
  170.3 2.3 slice-done.2
  172.6 2.7 copy.19
  175.6 5.9 %pad_maximum_fusion = (f32[64,3,4,2048]{3,0,2,1:T(8,128)}, f32[64,3,4,2048]{3,0,2,1:T(8,128)S(1)}) fusion(f32[64,3,3,2048]{3,0,2,1:T(8,128)S(1)} %copy.19, f32[64,3,1,2048]{3,0,2,1:T(8,128)S(1)} %convert_element_type.42, f32[64,3,4,2048]{3,2,1,0:T(4,128)S(1)} %bitcast.21, f32[4]{0:T(128)S(1)} %dynamic_slice.14), kind=kLoop, calls=%fused_computation.1 | loop fusion | flops 4718592 | bytes 25165840 | tf_op jit(solution)/shard_map/concatenate | solution.py:48
  181.5 2.8 copy-done
  184.4 1.3 collective-permute-start.1
  186.2 5.1 %slice.20 = f32[64,3,3,2048]{3,0,2,1:T(8,128)} slice(f32[64,3,4,2048]{3,0,2,1:T(8,128)} %copy-done), slice={[0:64], [0:3], [1:4], [0:2048]} | slice | bytes 9437184 | tf_op jit(solution)/shard_map/slice | solution.py:53
  191.3 6.7 %copy.11 = f32[64,3,4,2048]{3,2,1,0:T(4,128)} copy(f32[64,3,4,2048]{3,0,2,1:T(8,128)S(1)} %bitcast.23) | data formatting | bytes 12582912 | tf_op jit(solution)/shard_map/concatenate | solution.py:48
  198.0 8.0 %concatenate.11 = f32[64,24576]{1,0:T(8,128)} reshape(f32[64,3,4,2048]{3,2,1,0:T(4,128)} %copy.11) | data formatting | bytes 12582912 | tf_op jit(solution)/shard_map/concatenate | solution.py:48
  206.0 1.3 convert_element_type.43
  207.3 2.8 pad_maximum_fusion.1
  210.1 6.6 %copy.13 = f32[64,3,4,2048]{3,2,1,0:T(4,128)} copy(f32[64,3,4,2048]{3,0,2,1:T(8,128)S(1)} %pad_maximum_fusion.1) | data formatting | bytes 12582912 | tf_op jit(solution)/shard_map/concatenate | solution.py:53
  216.7 8.1 %concatenate.13 = f32[64,24576]{1,0:T(8,128)} reshape(f32[64,3,4,2048]{3,2,1,0:T(4,128)} %copy.13) | data formatting | bytes 12582912 | tf_op jit(solution)/shard_map/concatenate | solution.py:53
  224.8 6.4 %fusion.2 = f32[16,64]{1,0:T(8,128)S(1)} fusion(bf16[16,24576]{1,0:T(8,128)(2,1)} %copy-done.2, f32[64,24576]{1,0:T(8,128)} %concatenate.13, f32[64,24576]{1,0:T(8,128)} %concatenate.11, f32[24576]{0:T(1024)S(1)} %bitcast.26, f32[24576]{0:T(1024)S(1)} %bitcast.27, bf16[64,24576]{1,0:T(8,128)(2,1)S(1)} %copy-done.1), kind=kOutput, calls=%fused_computation.11 | convolution fusion | flops 62914560 | bytes 16715776 | tf_op jit(solution)/shard_map/dot_general | solution.py:59
  231.3 46.2 %psum.15 = f32[64,64]{1,0:T(8,128)S(1)} all-reduce(f32[64,64]{1,0:T(8,128)S(1)} %bitcast_multiply_fusion), channel_id=1, replica_groups=mesh['slab'=8,'field'=4] {'slab','field'}, use_global_device_ids=true, to_apply=%region_1.0 | all-reduce | flops 4096 | bytes 32768 | tf_op jit(solution)/shard_map/psum | solution.py:66
  (39 shorter events, 3.4 us)
Async XLA Ops:
  10.0 20.6 %all-to-all-start = ((bf16[1,2,3,32,2048]{4,2,1,0,3:T(4,128)(2,1)}), bf16[1,2,3,32,2048]{4,2,1,0,3:T(4,128)(2,1)S(1)}, u32[]{:S(2)}, u32[]{:S(2)}) async-start(bf16[1,2,3,32,2048]{4,2,1,0,3:T(4,128)(2,1)} %copy.7), calls=%async_computation | async-start | bytes 2097152 | tf_op jit(solution)/shard_map/all_to_all | solution.py:26
  15.1 140.3 %all-reduce.2.cloned.1.call-start = ((), (), s32[]{:S(2)}) async-start(), calls=%async_computation.1 | async-start | bytes 6291456 | tf_op jit(solution)/shard_map/psum | solution.py:34
  32.1 131.2 %copy-start.2 = (bf16[16,24576]{1,0:T(8,128)(2,1)}, bf16[16,24576]{1,0:T(8,128)(2,1)S(1)}, u32[]{:S(2)}) copy-start(bf16[16,24576]{1,0:T(8,128)(2,1)S(1)} %reshape.33) | copy-start | bytes 2359300
  34.8 135.4 %copy-start.3 = (s32[32]{0:T(128)S(1)}, s32[32]{0:T(128)}, u32[]{:S(2)}) copy-start(s32[32]{0:T(128)} %param.7) | copy-start | bytes 388
  168.2 7.1 %collective-permute-start = (bf16[64,3,1,2048]{3,0,2,1:T(8,128)(2,1)S(1)}, bf16[64,3,1,2048]{3,0,2,1:T(8,128)(2,1)S(1)}, u32[]{:S(2)}, u32[]{:S(2)}) collective-permute-start(bf16[64,3,1,2048]{3,0,2,1:T(8,128)(2,1)S(1)} %copy.20), channel_id=1, source_target_pairs={{0,4},{1,5},{2,6},{3,7},{4,8},{5,9},{6,10},{7,11},{8,12},{9,13},{1... | collective-permute-start | bytes 2359304 | tf_op jit(solution)/shard_map/ppermute | solution.py:10
  170.3 2.3 slice-start.2
  170.3 5.3 %slice-start = ((s8[6291456]{0:T(1024)(128)(4,1)}), s8[4194304]{0:T(1024)(128)(4,1)S(1)}, s32[]{:S(2)}) async-start(s8[6291456]{0:T(1024)(128)(4,1)} %bitcast.20), calls=%async_computation.2 | async-start | bytes 8388608
  172.6 2.9 %slice-start.1 = ((s8[6291456]{0:T(1024)(128)(4,1)}), s8[2097152]{0:T(1024)(128)(4,1)S(1)}, s32[]{:S(2)}) async-start(s8[6291456]{0:T(1024)(128)(4,1)} %bitcast.20), calls=%async_computation.3 | async-start | bytes 4194304
  181.5 2.8 copy-start
  181.5 9.9 %slice-start.3 = ((s8[6291456]{0:T(1024)(128)(4,1)}), s8[2097152]{0:T(1024)(128)(4,1)S(1)}, s32[]{:S(2)}) async-start(s8[6291456]{0:T(1024)(128)(4,1)} %bitcast.22), calls=%async_computation.5 | async-start | bytes 4194304
  184.4 21.6 %collective-permute-start.1 = (bf16[64,3,1,2048]{3,0,2,1:T(8,128)(2,1)S(1)}, bf16[64,3,1,2048]{3,0,2,1:T(8,128)(2,1)}, u32[]{:S(2)}, u32[]{:S(2)}) collective-permute-start(bf16[64,3,1,2048]{3,0,2,1:T(8,128)(2,1)S(1)} %slice.24), channel_id=1, source_target_pairs={{4,0},{5,1},{6,2},{7,3},{8,4},{9,5},{10,6},{11,7},{12,8},{13,9},{1... | collective-permute-start | bytes 2359304 | tf_op jit(solution)/shard_map/ppermute | solution.py:10
  186.2 5.1 %slice-start.4 = ((s8[6291456]{0:T(1024)(128)(4,1)}), s8[4194304]{0:T(1024)(128)(4,1)S(1)}, s32[]{:S(2)}) async-start(s8[6291456]{0:T(1024)(128)(4,1)} %bitcast.22), calls=%async_computation.6 | async-start | bytes 8388608
  216.7 8.1 %copy-start.1 = (bf16[64,24576]{1,0:T(8,128)(2,1)S(1)}, bf16[64,24576]{1,0:T(8,128)(2,1)}, u32[]{:S(2)}) copy-start(bf16[64,24576]{1,0:T(8,128)(2,1)} %all-reduce.2.cloned.1.call-done) | copy-start | bytes 9437188
Sparse Core Ops, SparseCore 0:
  34.9 120.4 all-reduce.1
where the time goes:
time: 286 us
  waiting for transfers between devices  135 us (47%)
  local copies, waits for them, and re-layouts  60.8 us (21%)
  blocking collectives  46.2 us (16%)
  between operations  14.2 us (5%)
  matrix products  10.9 us (4%)
  other arithmetic  10.2 us (4%)
  starting transfers between devices  8.43 us (3%)
    psum x1, waiting for transfers between devices, body(): lax.psum(partial_z.astype(jnp.bfloat16), 'field').astype(jnp.float32)  121 us
    psum x1, blocking collectives, body(): rows = lax.psum(stored_rows, ('slab', 'field'))  46.2 us
    concatenate x2, local copies, waits for them, and re-layouts, body(): above = jnp.concatenate([flux[:, :, 1:], upper], axis=2)  14.7 us
    concatenate x2, local copies, waits for them, and re-layouts, body(): below = jnp.concatenate([lower, sketched[:, :, :-1]], axis=2)  14.6 us
    all_to_all x1, waiting for transfers between devices, body(): lax.all_to_all(snaps, 'slab', split_axis=3, concat_axis=1, tiled=True)  14.4 us
    unnamed x23, local copies, waits for them, and re-layouts  9.04 us
    reshape x1, local copies, waits for them, and re-layouts, body(): sketched = sketched.reshape(sketch_cols, comps, planes_dev, cells)  7.87 us
    dot_general x1, matrix products, body(): lax.dot_general(flat, applied, (((1,), (1,)), ((), ())), preferred_elemen...  6.4 us
  transfers between devices with their start and end apart: 4, of which 2 were waited for; matrix products, arithmetic and copies ran while one was open for 8% of the time, Pallas kernels for 0%

commit v1 on v0

--- a/solution.py
+++ b/solution.py
@@ -2,6 +2,11 @@
 import jax.numpy as jnp
 from jax import lax
 from jax.sharding import PartitionSpec as P
+
+
+def add_all(array, axis):
+    blocks = lax.all_gather(array, axis)
+    return jnp.sum(blocks, axis=0)
 
 
 def from_behind(block, axis, distance):
@@ -63,7 +68,7 @@
     stored_rows = (blocks[:, None, None] * partial_rows[None, :, :]).reshape(
         total_snaps, sketch_cols
     )
-    rows = lax.psum(stored_rows, ("slab", "field"))
+    rows = add_all(stored_rows, ("slab", "field"))
     core = (
         jnp.dot(test_all.astype(jnp.float32).T, rows, precision=lax.Precision.HIGHEST) / total_snaps
     )

time: 286 us -> 324 us (1.13)
  blocking collectives: 46.2 us -> 83.4 us
    all_gather x0 -> x1, blocking collectives: none -> 83.4 us  [add_all(): blocks = lax.all_gather(array, axis)]
    psum x1 -> x0, blocking collectives: 46.2 us -> none  [body(): rows = lax.psum(stored_rows, ('slab', 'field'))]
  transfers between devices with their start and end apart: 4 -> 4, of which waited for: 2 -> 2; matrix products, arithmetic and copies ran while one was open for 8% -> 7% of each run, Pallas kernels for 0% -> 0%
where the time goes in v1:
time: 324 us; the launch traced here: 323 us
  waiting for transfers between devices  135 us (42%)
  blocking collectives  83.4 us (26%)
  local copies, waits for them, and re-layouts  60.8 us (19%)
  between operations  14.2 us (4%)
  matrix products  10.9 us (3%)
  other arithmetic  10.3 us (3%)
  starting transfers between devices  8.43 us (3%)
    psum x1, waiting for transfers between devices, body(): lax.psum(partial_z.astype(jnp.bfloat16), 'field').astype(jnp.float32)  121 us
    all_gather x1, blocking collectives, add_all(): blocks = lax.all_gather(array, axis)  83.4 us
    concatenate x2, local copies, waits for them, and re-layouts, body(): above = jnp.concatenate([flux[:, :, 1:], upper], axis=2)  14.7 us
    concatenate x2, local copies, waits for them, and re-layouts, body(): below = jnp.concatenate([lower, sketched[:, :, :-1]], axis=2)  14.6 us
    all_to_all x1, waiting for transfers between devices, body(): lax.all_to_all(snaps, 'slab', split_axis=3, concat_axis=1, tiled=True)  14.4 us
    unnamed x23, local copies, waits for them, and re-layouts  9.04 us
    reshape x1, local copies, waits for them, and re-layouts, body(): sketched = sketched.reshape(sketch_cols, comps, planes_dev, cells)  7.87 us
  transfers between devices with their start and end apart: 4, of which 2 were waited for; matrix products, arithmetic and copies ran while one was open for 7% of the time, Pallas kernels for 0%

profile of v1, /device:TPU:0, one launch (start us, length us, event | category | flops | bytes accessed | tf_op | source)
XLA Modules:
  0.0 323.0 jit_solution(4980729886656057329)
XLA Ops:
  7.2 2.8 copy.7
  10.0 5.2 %all-to-all-start = ((bf16[1,2,3,32,2048]{4,2,1,0,3:T(4,128)(2,1)}), bf16[1,2,3,32,2048]{4,2,1,0,3:T(4,128)(2,1)S(1)}, u32[]{:S(2)}, u32[]{:S(2)}) async-start(bf16[1,2,3,32,2048]{4,2,1,0,3:T(4,128)(2,1)} %copy.7), calls=%async_computation | async-start | bytes 2097152 | tf_op jit(solution)/shard_map/all_to_all | solution.py:31
  15.2 1.0 convolution_convert_fusion.1
  16.2 14.4 %all-to-all-done = bf16[1,2,3,32,2048]{4,2,1,0,3:T(4,128)(2,1)S(1)} async-done(((bf16[1,2,3,32,2048]{4,2,1,0,3:T(4,128)(2,1)}), bf16[1,2,3,32,2048]{4,2,1,0,3:T(4,128)(2,1)S(1)}, u32[]{:S(2)}, u32[]{:S(2)}) %all-to-all-start) | async-done | bytes 786464 | tf_op jit(solution)/shard_map/all_to_all | solution.py:31
  30.5 0.9 copy.18
  32.1 2.7 convolution_convert_fusion
  34.8 120.6 %all-reduce.2.cloned.1.call-done = bf16[64,24576]{1,0:T(8,128)(2,1)} async-done(((bf16[64,24576]{1,0:T(8,128)(2,1)}), bf16[64,24576]{1,0:T(8,128)(2,1)}) %all-reduce.2.cloned.1.call-update) | async-done | bytes 3145744 | tf_op jit(solution)/shard_map/psum | solution.py:39
  155.4 7.9 %reshape.65 = f32[64,3,4,2048]{3,2,1,0:T(4,128)} reshape(bf16[64,24576]{1,0:T(8,128)(2,1)} %all-reduce.2.cloned.1.call-done) | data formatting | bytes 9437184 | tf_op jit(solution)/shard_map/reshape | solution.py:40
  163.3 4.5 %slice.25 = bf16[64,3,1,2048]{3,2,1,0:T(2,128)(2,1)S(1)} slice(f32[64,3,4,2048]{3,2,1,0:T(4,128)} %reshape.65), slice={[0:64], [0:3], [3:4], [0:2048]} | slice | bytes 1572864 | tf_op jit(solution)/shard_map/slice | solution.py:51
  168.2 1.9 collective-permute-start
  170.3 2.3 slice-done.2
  172.6 2.7 copy.19
  175.6 5.9 %pad_maximum_fusion = (f32[64,3,4,2048]{3,0,2,1:T(8,128)}, f32[64,3,4,2048]{3,0,2,1:T(8,128)S(1)}) fusion(f32[64,3,3,2048]{3,0,2,1:T(8,128)S(1)} %copy.19, f32[64,3,1,2048]{3,0,2,1:T(8,128)S(1)} %convert_element_type.42, f32[64,3,4,2048]{3,2,1,0:T(4,128)S(1)} %bitcast.22, f32[4]{0:T(128)S(1)} %dynamic_slice.14), kind=kLoop, calls=%fused_computation.1 | loop fusion | flops 4718592 | bytes 25165840 | tf_op jit(solution)/shard_map/concatenate | solution.py:53
  181.5 2.8 copy-done
  184.4 1.3 collective-permute-start.1
  186.2 5.1 %slice.20 = f32[64,3,3,2048]{3,0,2,1:T(8,128)} slice(f32[64,3,4,2048]{3,0,2,1:T(8,128)} %copy-done), slice={[0:64], [0:3], [1:4], [0:2048]} | slice | bytes 9437184 | tf_op jit(solution)/shard_map/slice | solution.py:58
  191.3 6.7 %copy.11 = f32[64,3,4,2048]{3,2,1,0:T(4,128)} copy(f32[64,3,4,2048]{3,0,2,1:T(8,128)S(1)} %bitcast.24) | data formatting | bytes 12582912 | tf_op jit(solution)/shard_map/concatenate | solution.py:53
  198.0 8.0 %concatenate.11 = f32[64,24576]{1,0:T(8,128)} reshape(f32[64,3,4,2048]{3,2,1,0:T(4,128)} %copy.11) | data formatting | bytes 12582912 | tf_op jit(solution)/shard_map/concatenate | solution.py:53
  206.0 1.3 convert_element_type.43
  207.3 2.8 pad_maximum_fusion.1
  210.1 6.6 %copy.13 = f32[64,3,4,2048]{3,2,1,0:T(4,128)} copy(f32[64,3,4,2048]{3,0,2,1:T(8,128)S(1)} %pad_maximum_fusion.1) | data formatting | bytes 12582912 | tf_op jit(solution)/shard_map/concatenate | solution.py:58
  216.7 8.1 %concatenate.13 = f32[64,24576]{1,0:T(8,128)} reshape(f32[64,3,4,2048]{3,2,1,0:T(4,128)} %copy.13) | data formatting | bytes 12582912 | tf_op jit(solution)/shard_map/concatenate | solution.py:58
  224.8 6.4 %fusion.2 = f32[16,64]{1,0:T(8,128)S(1)} fusion(bf16[16,24576]{1,0:T(8,128)(2,1)} %copy-done.2, f32[64,24576]{1,0:T(8,128)} %concatenate.13, f32[64,24576]{1,0:T(8,128)} %concatenate.11, f32[24576]{0:T(1024)S(1)} %bitcast.27, f32[24576]{0:T(1024)S(1)} %bitcast.28, bf16[64,24576]{1,0:T(8,128)(2,1)S(1)} %copy-done.1), kind=kOutput, calls=%fused_computation.11 | convolution fusion | flops 62914560 | bytes 16715776 | tf_op jit(solution)/shard_map/dot_general | solution.py:64
  231.3 83.4 %all_gather.3 = f32[32,64,64]{2,1,0:T(8,128)S(1)} all-gather(f32[1,64,64]{2,1,0:T(8,128)S(1)} %bitcast_multiply_fusion), channel_id=1, replica_groups=mesh['slab'=8,'field'=4] {'slab','field'}, dimensions={0}, use_global_device_ids=true | all-gather | bytes 540672 | tf_op jit(solution)/shard_map/all_gather | solution.py:8
  (41 shorter events, 3.5 us)
Async XLA Ops:
  10.0 20.6 %all-to-all-start = ((bf16[1,2,3,32,2048]{4,2,1,0,3:T(4,128)(2,1)}), bf16[1,2,3,32,2048]{4,2,1,0,3:T(4,128)(2,1)S(1)}, u32[]{:S(2)}, u32[]{:S(2)}) async-start(bf16[1,2,3,32,2048]{4,2,1,0,3:T(4,128)(2,1)} %copy.7), calls=%async_computation | async-start | bytes 2097152 | tf_op jit(solution)/shard_map/all_to_all | solution.py:31
  15.1 140.3 %all-reduce.2.cloned.1.call-start = ((), (), s32[]{:S(2)}) async-start(), calls=%async_computation.1 | async-start | bytes 6291456 | tf_op jit(solution)/shard_map/psum | solution.py:39
  32.1 131.2 %copy-start.2 = (bf16[16,24576]{1,0:T(8,128)(2,1)}, bf16[16,24576]{1,0:T(8,128)(2,1)S(1)}, u32[]{:S(2)}) copy-start(bf16[16,24576]{1,0:T(8,128)(2,1)S(1)} %reshape.64) | copy-start | bytes 2359300
  34.8 135.4 %copy-start.3 = (s32[32]{0:T(128)S(1)}, s32[32]{0:T(128)}, u32[]{:S(2)}) copy-start(s32[32]{0:T(128)} %param.7) | copy-start | bytes 388
  168.2 7.1 %collective-permute-start = (bf16[64,3,1,2048]{3,0,2,1:T(8,128)(2,1)S(1)}, bf16[64,3,1,2048]{3,0,2,1:T(8,128)(2,1)S(1)}, u32[]{:S(2)}, u32[]{:S(2)}) collective-permute-start(bf16[64,3,1,2048]{3,0,2,1:T(8,128)(2,1)S(1)} %copy.20), channel_id=1, source_target_pairs={{0,4},{1,5},{2,6},{3,7},{4,8},{5,9},{6,10},{7,11},{8,12},{9,13},{1... | collective-permute-start | bytes 2359304 | tf_op jit(solution)/shard_map/ppermute | solution.py:15
  170.3 2.3 slice-start.2
  170.3 5.3 %slice-start = ((s8[6291456]{0:T(1024)(128)(4,1)}), s8[4194304]{0:T(1024)(128)(4,1)S(1)}, s32[]{:S(2)}) async-start(s8[6291456]{0:T(1024)(128)(4,1)} %bitcast.21), calls=%async_computation.2 | async-start | bytes 8388608
  172.6 2.9 slice-start.1
  181.5 2.8 copy-start
  181.5 9.9 %slice-start.3 = ((s8[6291456]{0:T(1024)(128)(4,1)}), s8[2097152]{0:T(1024)(128)(4,1)S(1)}, s32[]{:S(2)}) async-start(s8[6291456]{0:T(1024)(128)(4,1)} %bitcast.23), calls=%async_computation.5 | async-start | bytes 4194304
  184.4 21.6 %collective-permute-start.1 = (bf16[64,3,1,2048]{3,0,2,1:T(8,128)(2,1)S(1)}, bf16[64,3,1,2048]{3,0,2,1:T(8,128)(2,1)}, u32[]{:S(2)}, u32[]{:S(2)}) collective-permute-start(bf16[64,3,1,2048]{3,0,2,1:T(8,128)(2,1)S(1)} %slice.24), channel_id=1, source_target_pairs={{4,0},{5,1},{6,2},{7,3},{8,4},{9,5},{10,6},{11,7},{12,8},{13,9},{1... | collective-permute-start | bytes 2359304 | tf_op jit(solution)/shard_map/ppermute | solution.py:15
  186.2 5.1 %slice-start.4 = ((s8[6291456]{0:T(1024)(128)(4,1)}), s8[4194304]{0:T(1024)(128)(4,1)S(1)}, s32[]{:S(2)}) async-start(s8[6291456]{0:T(1024)(128)(4,1)} %bitcast.23), calls=%async_computation.6 | async-start | bytes 8388608
  216.7 8.1 %copy-start.1 = (bf16[64,24576]{1,0:T(8,128)(2,1)S(1)}, bf16[64,24576]{1,0:T(8,128)(2,1)}, u32[]{:S(2)}) copy-start(bf16[64,24576]{1,0:T(8,128)(2,1)} %all-reduce.2.cloned.1.call-done) | copy-start | bytes 9437188
Sparse Core Ops, SparseCore 0:
  34.9 120.4 all-reduce.1
